TPU v7x, 768 devices: a whole 4x8x12 slice. The times are simulated.
768 devices in a mesh: row: 192 (over x, z, y_hi, core), col: 4 (over y_lo).
Axes of the slice: x: 4, y: 8 (y_hi: 2, y_lo: 4; y = y_hi * 4 + y_lo), z: 12, core: 2. Of those that a mesh axis runs over, the one named last changes fastest.
Arguments:
- out_grad: bfloat16 [1536, 8192], P('row', 'col'), may hold values from -6 to 6
- down_weight: bfloat16 [24576, 8192], P('row', 'col'), may hold values from -0.0546875 to 0.0546875
- block_mask: int32 [192, 64], P('row', 'col'), may hold values from 0 to 1, as said below
- gate_act: bfloat16 [1536, 24576], P('col', 'row'), may hold values from -6 to 6
- up_act: bfloat16 [1536, 24576], P('col', 'row'), may hold values from -6 to 6
Outputs:
- grad_gate: bfloat16 [1536, 24576], P('col', 'row')
- grad_up: bfloat16 [1536, 24576], P('col', 'row')
- grad_down: bfloat16 [24576, 8192], P('row', 'col')
Inputs may be any that keep to these rules, and one draw needn't show every extreme that they name: `block_mask`: in each block row, every aligned group of 16 blocks along the features holds between 4 and 12 ones, and some group holds exactly 12.
All inputs are finite; a program needn't handle non-finite values.
Results may differ from a plain program's by a relative error of at most 0.0049.
Values may be sent and summed in bfloat16 or wider, within the bound.
A program may use at most 32 MiB of HBM per device.

v0:
```python
import jax
import jax.numpy as jnp
from jax import lax
from jax.sharding import PartitionSpec as P

BLK = 128


def shards(out_grad, down_weight, block_mask, gate_act, up_act):
    gate_f = gate_act.astype(jnp.float32)
    up_f = up_act.astype(jnp.float32)
    sig = jax.nn.sigmoid(gate_f)
    hidden = (gate_f * sig * up_f).astype(jnp.bfloat16)
    all_hidden = lax.all_gather(hidden, "col", axis=0, tiled=True)
    expand = jnp.repeat(jnp.repeat(block_mask.astype(jnp.bfloat16), BLK, 0), BLK, 1)
    kept = down_weight * expand
    piece = lax.all_gather(out_grad, "row", axis=0, tiled=True)
    wgrad = lax.dot_general(
        all_hidden, piece, (((0,), (0,)), ((), ())), preferred_element_type=jnp.float32
    )
    term = lax.dot_general(
        piece, kept, (((1,), (1,)), ((), ())), preferred_element_type=jnp.float32
    )
    partial_value = term
    wgrad, partial_value = (wgrad, partial_value)
    grad_down = (wgrad * expand.astype(jnp.float32)).astype(jnp.bfloat16)
    grad_hidden = lax.psum_scatter(partial_value, "col", scatter_dimension=0, tiled=True)
    grad_up = (grad_hidden * gate_f * sig).astype(jnp.bfloat16)
    grad_gate = (grad_hidden * up_f * sig * (1.0 + gate_f * (1.0 - sig))).astype(jnp.bfloat16)
    return (grad_gate, grad_up, grad_down)


def solution(mesh):
    in_specs = (P("row", "col"), P("row", "col"), P("row", "col"), P("col", "row"), P("col", "row"))
    out_specs = (P("col", "row"), P("col", "row"), P("row", "col"))
    return jax.shard_map(shards, mesh=mesh, in_specs=in_specs, out_specs=out_specs, check_vma=False)
```

profile of v0, /device:TPU:1, one launch (start us, length us, event | category | flops | bytes accessed | tf_op | source)
XLA Modules:
  0.0 274.4 jit_solution(2007317355781065098)
XLA Ops:
  7.2 0.0 copy-start
  7.2 0.0 copy-start.1
  7.2 0.0 all-gather.2.cloned.1.call-start
  7.2 0.7 all-gather.2.cloned.1.call-update
  7.9 0.0 reduce-scatter.2.cloned.1.call-start
  8.0 0.7 convert_bitcast_fusion
  8.6 0.1 bitcast_convert_fusion
  8.7 207.6 %all-gather.2.cloned.1.call-done = bf16[1536,2048]{1,0:T(8,128)(2,1)} async-done(((bf16[8,2048]{1,0:T(8,128)(2,1)}), bf16[1536,2048]{1,0:T(8,128)(2,1)}) %all-gather.2.cloned.1.call-update) | async-done | bytes 6291472 | tf_op jit(solution)/shard_map/all_gather | solution.py:17
  216.3 6.1 %convolution_bitcast_fusion = f32[1536,128]{0,1:T(8,128)} fusion(bf16[1536,2048]{1,0:T(8,128)(2,1)} %all-gather.2.cloned.1.call-done, bf16[128,2048]{1,0:T(8,128)(2,1)} %param.6, bf16[2048]{0:T(1024)(128)(2,1)S(1)} %get-tuple-element.10), kind=kOutput, calls=%fused_computation.1 | convolution fusion | flops 805568512 | bytes 7606272 | tf_op jit(solution)/shard_map/dot_general | solution.py:21
  222.3 0.0 reduce-scatter.2.cloned.1.call-update
  222.3 0.0 copy-done
  222.4 0.1 copy.9
  222.5 0.0 copy-done.1
  222.5 0.1 copy.8
  222.6 25.1 %reduce-scatter.2.cloned.1.call-done = f32[384,128]{0,1:T(8,128)} async-done(((f32[1536,128]{0,1:T(8,128)}), f32[384,128]{0,1:T(8,128)}) %reduce-scatter.2.cloned.1.call-update) | async-done | bytes 196624 | tf_op jit(solution)/shard_map/reduce_scatter | solution.py:27
  247.7 1.1 fusion.12
  248.7 0.8 copy.10
  249.5 0.8 copy.11
  250.2 12.8 %all_gather.7 = bf16[1536,128]{0,1:T(8,128)(2,1)S(1)} all-gather(bf16[384,128]{0,1:T(8,128)(2,1)S(1)} %get-tuple-element.8), channel_id=1, replica_groups=mesh['row'=192,'col'=4] {'col'}, dimensions={0}, use_global_device_ids=true | all-gather | bytes 491520 | tf_op jit(solution)/shard_map/all_gather | solution.py:14
  263.0 4.6 %fusion = bf16[128,2048]{1,0:T(8,128)(2,1)} fusion(bf16[1536,128]{0,1:T(8,128)(2,1)S(1)} %all_gather.7, bf16[1536,2048]{1,0:T(8,128)(2,1)} %all-gather.2.cloned.1.call-done, f32[2048]{0:T(1024)S(1)} %get-tuple-element.9), kind=kOutput, calls=%fused_computation.2 | convolution fusion | flops 805830656 | bytes 7217152 | tf_op jit(solution)/shard_map/dot_general | solution.py:18
Async XLA Ops:
  7.2 215.2 %copy-start = (bf16[384,128]{1,0:T(8,128)(2,1)S(1)}, bf16[384,128]{1,0:T(8,128)(2,1)}, u32[]{:S(2)}) copy-start(bf16[384,128]{1,0:T(8,128)(2,1)} %param.8) | copy-start | bytes 294916
  7.2 215.3 %copy-start.1 = (bf16[384,128]{1,0:T(8,128)(2,1)S(1)}, bf16[384,128]{1,0:T(8,128)(2,1)}, u32[]{:S(2)}) copy-start(bf16[384,128]{1,0:T(8,128)(2,1)} %param.9) | copy-start | bytes 294916
  7.2 209.1 %all-gather.2.cloned.1.call-start = ((), (), s32[]{:S(2)}) async-start(), calls=%async_computation.1 | async-start | bytes 6324224 | tf_op jit(solution)/shard_map/all_gather | solution.py:17
  7.9 239.8 %reduce-scatter.2.cloned.1.call-start = ((), (), s32[]{:S(2)}) async-start(), calls=%async_computation.2 | async-start | bytes 983040 | tf_op jit(solution)/shard_map/reduce_scatter | solution.py:27
Sparse Core Ops, SparseCore 0:
  13.6 202.6 all-gather.1
  222.5 25.1 reduce-scatter.1
where the time goes:
time: 277 us; the launch traced here: 274 us
  waiting for transfers between devices  233 us (84%)
  between operations  14.1 us (5%)
  blocking collectives  12.8 us (5%)
  matrix products  10.6 us (4%)
    all_gather x1, waiting for transfers between devices, shards(): piece = lax.all_gather(out_grad, 'row', axis=0, tiled=True)  208 us
    reduce_scatter x1, waiting for transfers between devices, shards(): lax.psum_scatter(partial_value, 'col', scatter_dimension=0, tiled=True)  25.1 us
    all_gather x1, blocking collectives, shards(): all_hidden = lax.all_gather(hidden, 'col', axis=0, tiled=True)  12.8 us
    dot_general x1, matrix products, shards(): lax.dot_general(piece, kept, (((1,), (1,)), ((), ())), preferred_element_...  6.05 us
  transfers between devices with their start and end apart: 2, of which 2 were waited for; matrix products, arithmetic and copies ran while one was open for 0% of the time, Pallas kernels for 0%

commit v1 on v0

v1 whole, which is shorter than its diff:
```python
import jax
import jax.numpy as jnp
from jax import lax
from jax.experimental import pallas as pl
from jax.experimental.pallas import tpu as pltpu
from jax.sharding import PartitionSpec as P

MESH = pl.DeviceIdType.MESH
F32 = jnp.float32
BF16 = jnp.bfloat16

BLK = 128
NX, NZ, NH, NC, NCOL = 4, 12, 2, 2, 4
HALF = 1024
FA = 384
FB = HALF - FA
ROWS = 32
STEPS = NZ // 2
GROUPS = STEPS + 1


def slots(g):
    if g == 0:
        return 0, 1
    if g == STEPS:
        return NZ - 1, NZ
    return 2 * g - 1, 2 * g + 1


def slot_offset(r):
    if r == 0:
        return 0
    if r == NZ - 1:
        return STEPS
    s = (r + 1) // 2
    return -s if r % 2 else s


def kernel(
    x_ref, w_ref, mask_ref, gate_ref, up_ref,
    gg_ref, gu_ref, gd_ref,
    pack, quart, ga, gb, wm, hs, acc, tbuf, pbuf, rbuf,
    init_s, init_r, ax_s, ax_r, az_s, az_r, bz_s, bz_r, bx_s, bx_r,
    sa_s, sa_r, sb_s, sb_r, h_s, h_r, p_s, p_r,
):
    row, col = lax.axis_index("row"), lax.axis_index("col")
    c = lax.rem(row, NC)
    h = lax.rem(row // NC, NH)
    z0 = lax.rem(row // (NC * NH), NZ)
    x0 = row // (NC * NH * NZ)
    d = 1 - 2 * c

    def device(x, z, hh, cc):
        return (((x * NZ + z) * NH + hh) * NC + cc, col)

    xf = device(lax.rem(x0 + d + NX, NX), z0, h, c)
    xb = device(lax.rem(x0 - d + NX, NX), z0, h, c)
    zf = device(x0, lax.rem(z0 + d + NZ, NZ), h, c)
    zb = device(x0, lax.rem(z0 - d + NZ, NZ), h, c)
    sib = device(x0, z0, h, 1 - c)
    far0 = device(x0, z0, 1 - h, c)
    far1 = device(x0, z0, 1 - h, 1 - c)
    cols = [(row, lax.rem(col + k, NCOL)) for k in range(1, NCOL)]

    def copy(src, dst, send, recv, to):
        return pltpu.make_async_remote_copy(
            src_ref=src, dst_ref=dst, send_sem=send, recv_sem=recv,
            device_id=to, device_id_type=MESH,
        )

    sent = []

    def start(cp):
        cp.start()
        sent.append(cp)

    barrier = pltpu.get_barrier_semaphore()
    peers = [sib, far0, far1, xf, xb, zf, zb] + cols
    for peer in peers:
        pl.semaphore_signal(barrier, inc=1, device_id=peer, device_id_type=MESH)

    xs = x_ref[...].astype(F32)
    q = HALF // 2
    for cc in range(NC):
        pack[cc] = jnp.concatenate(
            [xs[:, cc * HALF:cc * HALF + q], xs[:, cc * HALF + q:(cc + 1) * HALF]], axis=0
        ).astype(BF16)
    pl.semaphore_wait(barrier, len(peers))

    first = [
        copy(pack.at[1 - c], quart.at[h, c], init_s.at[0], init_r.at[0], sib),
        copy(pack.at[c], quart.at[h, c], init_s.at[1], init_r.at[1], far0),
        copy(pack.at[1 - c], quart.at[h, c], init_s.at[2], init_r.at[2], far1),
    ]
    for cp in first:
        start(cp)

    quart[h, c] = pack[c]
    for b in range(2 * HALF // BLK):
        lanes = slice(b * BLK, (b + 1) * BLK)
        wm[:, lanes] = (w_ref[:, lanes].astype(F32) * mask_ref[0, b].astype(F32)).astype(BF16)
    places = []
    for r in range(NZ):
        z = lax.rem(z0 + slot_offset(r) + NZ, NZ)
        places.append(pl.ds(pl.multiple_of(z * ROWS, ROWS), ROWS))
    for r in range(NZ):
        gate = gate_ref[places[r], :].astype(F32)
        up = up_ref[places[r], :].astype(F32)
        hs[col, r] = (gate * jax.nn.sigmoid(gate) * up).astype(BF16)

    for cp in first:
        cp.wait_recv()
    for hh in range(NH):
        parts = []
        for cc in range(NC):
            v = quart[hh, cc].astype(F32)
            parts.append(jnp.concatenate([v[0:8], v[8:16]], axis=1))
        block = jnp.concatenate(parts, axis=0).astype(BF16)
        ga[c, x0, 0, 16 * hh:16 * hh + 16, :] = block[:, :FA]
        gb[c, x0, 0, 16 * hh:16 * hh + 16, :] = block[:, FA:]

    def zslot(way, s):
        if s == 0:
            return 0
        if s == STEPS:
            return NZ - 1
        return 2 * s - 1 + c if way == 0 else 2 * s - c

    ways = [(zf, STEPS), (zb, STEPS - 1)]

    def bz(way, s):
        src, dst = zslot(way, s - 1), zslot(way, s)
        i = way * STEPS + s - 1
        return copy(gb.at[c, x0, src], gb.at[c, x0, dst], bz_s.at[i], bz_r.at[i], ways[way][0])

    def az(way, s):
        src, dst = zslot(way, s - 1), zslot(way, s)
        i = way * STEPS + s - 1
        return copy(ga.at[c, :, src], ga.at[c, :, dst], az_s.at[i], az_r.at[i], ways[way][0])

    xprev = lax.rem(x0 - d + NX, NX)

    def ax(k):
        xs_ = xprev if k == 1 else x0
        ref = ga.at[c, xs_, 0]
        return copy(ref, ref, ax_s.at[k], ax_r.at[k], xb if k == 2 else xf)

    def bx(g, k):
        lo, hi = slots(g)
        xs_ = xprev if k == 1 else x0
        ref = gb.at[c, xs_, pl.ds(lo, hi - lo)]
        return copy(ref, ref, bx_s.at[g, k], bx_r.at[g, k], xb if k == 2 else xf)

    def sa(g):
        lo, hi = slots(g)
        ref = ga.at[c, :, pl.ds(lo, hi - lo)]
        return copy(ref, ref, sa_s.at[g], sa_r.at[g], sib)

    def sb(g):
        lo, hi = slots(g)
        ref = gb.at[c, :, pl.ds(lo, hi - lo)]
        return copy(ref, ref, sb_s.at[g], sb_r.at[g], sib)

    def hid(k):
        ref = hs.at[col]
        return copy(ref, ref, h_s.at[k], h_r.at[k], cols[k])

    def part(g, k):
        lo, hi = slots(g)
        dest = lax.rem(col + k + 1, NCOL)
        return copy(
            pbuf.at[dest, pl.ds(lo, hi - lo)], rbuf.at[k, pl.ds(lo, hi - lo)],
            p_s.at[g, k], p_r.at[g, k], cols[k],
        )

    def compute(g):
        sa(g).wait_recv()
        sb(g).wait_recv()
        lo, hi = slots(g)
        tokens = NX * (hi - lo) * ROWS
        hid_g = hs[:, lo:hi].reshape(tokens, BLK)
        term = None
        for cc in range(NC):
            for buf, at, n in ((ga, 0, FA), (gb, FA, FB)):
                v = buf[cc, :, lo:hi].reshape(tokens, n)
                lanes = slice(cc * HALF + at, cc * HALF + at + n)
                t = lax.dot_general(
                    v, wm[:, lanes], (((1,), (1,)), ((), ())), preferred_element_type=F32
                )
                term = t if term is None else term + t
        term = term.reshape(NX, hi - lo, ROWS, BLK)
        tbuf[:, lo:hi] = term
        pbuf[:, lo:hi] = term.astype(BF16)
        for k in range(NCOL - 1):
            start(part(g, k))
        for cc in range(NC):
            for buf, at, n in ((ga, 0, FA), (gb, FA, FB)):
                v = buf[cc, :, lo:hi].reshape(tokens, n)
                lanes = slice(cc * HALF + at, cc * HALF + at + n)
                t = lax.dot_general(
                    hid_g, v, (((0,), (0,)), ((), ())), preferred_element_type=F32
                )
                acc[:, lanes] = t if g == 0 else acc[:, lanes] + t

    for way in range(2):
        start(bz(way, 1))
    start(ax(0))
    start(ax(2))
    start(bx(0, 0))
    start(bx(0, 2))
    for k in range(NCOL - 1):
        start(hid(k))
    ax(0).wait_recv()
    start(ax(1))
    ax(2).wait_recv()
    ax(1).wait_recv()
    for way in range(2):
        start(az(way, 1))
    start(sa(0))

    for s in range(1, STEPS + 1):
        for way in range(2):
            if s <= ways[way][1]:
                bz(way, s).wait_recv()
                if s < ways[way][1]:
                    start(bz(way, s + 1))
        start(bx(s, 0))
        start(bx(s, 2))
        bx(s - 1, 0).wait_recv()
        start(bx(s - 1, 1))
        for way in range(2):
            if s <= ways[way][1]:
                az(way, s).wait_recv()
                if s < ways[way][1]:
                    start(az(way, s + 1))
        start(sa(s))
        bx(s - 1, 2).wait_recv()
        bx(s - 1, 1).wait_recv()
        start(sb(s - 1))
        if s == 2:
            for k in range(NCOL - 1):
                hid(k).wait_recv()
        if s >= 2:
            compute(s - 2)
    last = STEPS
    bx(last, 0).wait_recv()
    start(bx(last, 1))
    compute(last - 1)
    bx(last, 2).wait_recv()
    bx(last, 1).wait_recv()
    start(sb(last))
    compute(last)

    for b in range(2 * HALF // BLK):
        lanes = slice(b * BLK, (b + 1) * BLK)
        gd_ref[:, lanes] = (acc[:, lanes] * mask_ref[0, b].astype(F32)).astype(BF16)
    for g in range(GROUPS):
        for k in range(NCOL - 1):
            part(g, k).wait_recv()
    for r in range(NZ):
        gate = gate_ref[places[r], :].astype(F32)
        up = up_ref[places[r], :].astype(F32)
        sig = jax.nn.sigmoid(gate)
        gh = tbuf[col, r]
        for k in range(NCOL - 1):
            gh = gh + rbuf[k, r].astype(F32)
        gu_ref[places[r], :] = (gh * gate * sig).astype(BF16)
        gg_ref[places[r], :] = (gh * up * sig * (1.0 + gate * (1.0 - sig))).astype(BF16)
    for cp in sent:
        cp.wait_send()


def shards(out_grad, down_weight, block_mask, gate_act, up_act):
    vmem = pl.BlockSpec(memory_space=pltpu.VMEM)
    smem = pl.BlockSpec(memory_space=pltpu.SMEM)
    dma = pltpu.SemaphoreType.DMA
    units = down_weight.shape[0]
    rings = 2 * STEPS - 1
    scratch = [
        pltpu.VMEM((NC, 16, HALF // 2), BF16),
        pltpu.VMEM((NH, NC, 16, HALF // 2), BF16),
        pltpu.VMEM((NC, NX, NZ, ROWS, FA), BF16),
        pltpu.VMEM((NC, NX, NZ, ROWS, FB), BF16),
        pltpu.VMEM((units, NC * HALF), BF16),
        pltpu.VMEM((NX, NZ, ROWS, units), BF16),
        pltpu.VMEM((units, NC * HALF), F32),
        pltpu.VMEM((NX, NZ, ROWS, units), F32),
        pltpu.VMEM((NX, NZ, ROWS, units), BF16),
        pltpu.VMEM((NCOL - 1, NZ, ROWS, units), BF16),
    ]
    for shape in ((3,), (3,), (rings,), (rings,), (GROUPS, 3), (GROUPS,), (GROUPS,), (NCOL - 1,), (GROUPS, NCOL - 1)):
        scratch += [dma(shape), dma(shape)]
    return pl.pallas_call(
        kernel,
        out_shape=(
            jax.ShapeDtypeStruct(gate_act.shape, BF16),
            jax.ShapeDtypeStruct(up_act.shape, BF16),
            jax.ShapeDtypeStruct(down_weight.shape, BF16),
        ),
        in_specs=[vmem, vmem, smem, vmem, vmem],
        out_specs=(vmem, vmem, vmem),
        scratch_shapes=scratch,
        compiler_params=pltpu.CompilerParams(
            collective_id=0, has_side_effects=True, vmem_limit_bytes=40 * 1024 * 1024
        ),
    )(out_grad, down_weight, block_mask, gate_act, up_act)


def solution(mesh):
    in_specs = (P("row", "col"), P("row", "col"), P("row", "col"), P("col", "row"), P("col", "row"))
    out_specs = (P("col", "row"), P("col", "row"), P("row", "col"))
    return jax.shard_map(shards, mesh=mesh, in_specs=in_specs, out_specs=out_specs, check_vma=False)
```

time: 277 us -> 79.6 us (0.29)
  waiting for transfers between devices: 233 us -> 0 us
  Pallas kernels: 0 us -> 71.4 us
  between operations: 14.1 us -> 0.65 us
  blocking collectives: 12.8 us -> 0 us
  matrix products: 10.6 us -> 0 us
  local copies, waits for them, and re-layouts: 1.76 us -> 6.31 us
    all_gather x1 -> x0, waiting for transfers between devices: 208 us -> none  [shards(): piece = lax.all_gather(out_grad, 'row', axis=0, tiled=True)]
    pallas_call x0 -> x1, Pallas kernels: none -> 71.4 us  [shards(): pl.pallas_call(kernel, out_shape=(jax.ShapeDtypeStruct(gate_act.shape, BF...]
    reduce_scatter x1 -> x0, waiting for transfers between devices: 25.1 us -> none  [shards(): lax.psum_scatter(partial_value, 'col', scatter_dimension=0, tiled=True)]
    all_gather x1 -> x0, blocking collectives: 12.8 us -> none  [shards(): all_hidden = lax.all_gather(hidden, 'col', axis=0, tiled=True)]
    dot_general x2 -> x0, matrix products: 10.6 us -> none  [the longest x1 6.05 us: shards(): lax.dot_general(piece, kept, (((1,), (1,)), ((), ())), preferred_element_...]
    unnamed x8 -> x13, local copies, waits for them, and re-layouts: 1.76 us -> 6.31 us
  transfers between devices with their start and end apart: 2 -> 0, of which waited for: 2 -> 0; matrix products, arithmetic and copies ran while one was open for 0% -> 0% of each run, Pallas kernels for 0% -> 0%
where the time goes in v1:
time: 79.6 us; the launch traced here: 78.4 us
  Pallas kernels  71.4 us (90%)
  local copies, waits for them, and re-layouts  6.31 us (8%)
    pallas_call x1, Pallas kernels, shards(): pl.pallas_call(kernel, out_shape=(jax.ShapeDtypeStruct(gate_act.shape, BF...  71.4 us
    unnamed x13, local copies, waits for them, and re-layouts  6.31 us

profile of v1, /device:TPU:1, one launch (start us, length us, event | category | flops | bytes accessed | tf_op | source)
XLA Modules:
  0.0 78.4 jit_solution(5227570799367975945)
XLA Ops:
  0.6 0.0 copy-start
  0.6 1.0 %copy-done = bf16[128,2048]{1,0:T(8,128)(2,1)S(1)} copy-done((bf16[128,2048]{1,0:T(8,128)(2,1)S(1)}, bf16[128,2048]{1,0:T(8,128)(2,1)}, u32[]{:S(2)}) %copy-start) | copy-done | bytes 524312
  1.7 0.0 copy-start.1
  1.7 0.9 %copy-done.1 = bf16[384,128]{1,0:T(8,128)(2,1)S(1)} copy-done((bf16[384,128]{1,0:T(8,128)(2,1)S(1)}, bf16[384,128]{1,0:T(8,128)(2,1)}, u32[]{:S(2)}) %copy-start.1) | copy-done | bytes 98328
  2.6 0.0 copy-start.2
  2.6 0.9 %copy-done.2 = bf16[384,128]{1,0:T(8,128)(2,1)S(1)} copy-done((bf16[384,128]{1,0:T(8,128)(2,1)S(1)}, bf16[384,128]{1,0:T(8,128)(2,1)}, u32[]{:S(2)}) %copy-start.2) | copy-done | bytes 98328
  3.5 0.0 copy-start.3
  3.5 0.8 copy-done.3
  4.2 0.0 copy-start.4
  4.2 0.7 copy-done.4
  4.9 71.4 %shard_map.76 = (bf16[384,128]{1,0:T(8,128)(2,1)S(1)}, bf16[384,128]{1,0:T(8,128)(2,1)S(1)}, bf16[128,2048]{1,0:T(8,128)(2,1)S(1)}) custom-call(bf16[8,2048]{1,0:T(8,128)(2,1)S(1)} %copy-done.3, bf16[128,2048]{1,0:T(8,128)(2,1)S(1)} %copy-done, s32[1,16]{1,0:T(1,128)S(1)} %copy-done.4, bf16[384,128]{1,0:T(8,128)(2,1)S(1)} %copy-done.1, ...), custom_call_target="tpu_custom_call" | custom-call | tf_op jit(solution)/shard_map/pallas_call | solution.py:293
  76.3 0.6 copy.11
  76.9 0.6 copy.12
  77.6 0.8 %copy.13 = bf16[128,2048]{1,0:T(8,128)(2,1)} copy(bf16[128,2048]{1,0:T(8,128)(2,1)S(1)} %get-tuple-element.8) | data formatting | bytes 1048576
Async XLA Ops:
  0.6 1.0 %copy-start = (bf16[128,2048]{1,0:T(8,128)(2,1)S(1)}, bf16[128,2048]{1,0:T(8,128)(2,1)}, u32[]{:S(2)}) copy-start(bf16[128,2048]{1,0:T(8,128)(2,1)} %w_ref.1) | copy-start | bytes 1572868
  1.7 0.9 %copy-start.1 = (bf16[384,128]{1,0:T(8,128)(2,1)S(1)}, bf16[384,128]{1,0:T(8,128)(2,1)}, u32[]{:S(2)}) copy-start(bf16[384,128]{1,0:T(8,128)(2,1)} %gate_ref.1) | copy-start | bytes 294916
  2.6 0.9 %copy-start.2 = (bf16[384,128]{1,0:T(8,128)(2,1)S(1)}, bf16[384,128]{1,0:T(8,128)(2,1)}, u32[]{:S(2)}) copy-start(bf16[384,128]{1,0:T(8,128)(2,1)} %up_ref.1) | copy-start | bytes 294916
  3.5 0.8 copy-start.3
  4.2 0.7 copy-start.4

commit v2 on v0

v2 whole, which is shorter than its diff:
```python
import heapq

import jax
import jax.numpy as jnp
from jax import lax
from jax.experimental import pallas as pl
from jax.experimental.pallas import tpu as pltpu
from jax.sharding import PartitionSpec as P

MESH = pl.DeviceIdType.MESH
F32 = jnp.float32
BF16 = jnp.bfloat16

BLK = 128
NX, NZ, NH, NC, NCOL = 4, 12, 2, 2, 4
TOK = 8
PACK = 2 * TOK
HALF = 1024
ROWS = NH * NC * TOK
STEPS = NZ // 2
GROUPS = STEPS + 1
WAYS = (STEPS, STEPS - 1)

STREAMS = (
    (0, "zx", 384, 640),
    (0, "xz", 0, 384),
    (1, "zx", 384, 640),
    (1, "xz", 0, 384),
)


def slots(g):
    if g == 0:
        return 0, 1
    if g == STEPS:
        return NZ - 1, NZ
    return 2 * g - 1, 2 * g + 1


def slot_offset(r):
    if r == 0:
        return 0
    if r == NZ - 1:
        return STEPS
    s = (r + 1) // 2
    return -s if r % 2 else s


def make_plan():
    rate = {"z": 91e3, "x": 91e3, "sib": 400e3}
    free = {"z": 0.0, "x": 0.0, "sib": 0.0}
    latency, issue = 0.9, 0.06
    ops, arrivals = [], []
    now = 0.0
    seen = {}
    ready = [0] * GROUPS
    todo = []

    def start(msg, kind, size):
        nonlocal now
        ops.append(("start", msg))
        now += issue
        free[kind] = max(free[kind], now) + size / rate[kind]
        heapq.heappush(arrivals, (free[kind] + latency, msg))

    def size(i, slots_, xs):
        return slots_ * xs * PACK * STREAMS[i][3] * 2

    def nslots(g):
        lo, hi = slots(g)
        return hi - lo

    def send_z(i, way, s):
        start(("z", i, way, s), "z", size(i, 1, 1 if STREAMS[i][1] == "zx" else NX))

    def send_x(i, g, k):
        start(("x", i, g, k), "x", size(i, nslots(g), 1))

    def send_sib(i, g):
        start(("sib", i, g), "sib", size(i, nslots(g), NX))

    def begin(i):
        if STREAMS[i][1] == "zx":
            send_z(i, 0, 1)
            send_z(i, 1, 1)
        send_x(i, 0, 0)
        send_x(i, 0, 2)

    def count(key, full):
        seen[key] = seen.get(key, 0) + 1
        return seen[key] == full

    for i in (0, 1):
        begin(i)
    ops.append(("prepare",))
    now += 1.5
    heapq.heappush(arrivals, (5.5, ("far",)))
    heapq.heappush(arrivals, (9.0, ("hid",)))
    done = 0
    while arrivals or todo:
        if todo and (not arrivals or arrivals[0][0] > now):
            g = todo.pop(0)
            ops.append(("compute", g))
            now += 0.6 if g in (0, STEPS) else 1.0
            continue
        at, msg = heapq.heappop(arrivals)
        now = max(now, at) + issue
        if msg[0] == "sib":
            ready[msg[2]] += 1
            while done < GROUPS and ready[done] == len(STREAMS) and seen.get("hid"):
                todo.append(done)
                done += 1
            continue
        ops.append(("wait", msg))
        if msg[0] == "far":
            for i in (2, 3):
                begin(i)
        elif msg[0] == "hid":
            seen["hid"] = 1
        elif msg[0] == "z":
            _, i, way, s = msg
            if s < WAYS[way]:
                send_z(i, way, s + 1)
            if count(("z", i, s), 1 if s == STEPS else 2):
                if STREAMS[i][1] == "zx":
                    send_x(i, s, 0)
                    send_x(i, s, 2)
                else:
                    send_sib(i, s)
        else:
            _, i, g, k = msg
            if k == 0:
                send_x(i, g, 1)
            if count(("x", i, g), 3):
                if STREAMS[i][1] == "xz":
                    send_z(i, 0, 1)
                    send_z(i, 1, 1)
                send_sib(i, g)
    return ops, now


def kernel(
    x_hbm, w_hbm, mask_hbm, gate_hbm, up_hbm,
    gg_ref, gu_ref, gd_ref,
    xv, wv, mask, gv, uv, data, wm, hs, acc, tbuf, pbuf, rbuf,
    in_s, far_s, far_r, z_s, z_r, x_s, x_r, sib_s, sib_r, h_s, h_r, p_s, p_r,
):
    row, col = lax.axis_index("row"), lax.axis_index("col")
    c = lax.rem(row, NC)
    h = lax.rem(row // NC, NH)
    z0 = lax.rem(row // (NC * NH), NZ)
    x0 = row // (NC * NH * NZ)
    d = 1 - 2 * c
    xprev = lax.rem(x0 - d + NX, NX)

    def device(x, z, hh, cc):
        return (((x * NZ + z) * NH + hh) * NC + cc, col)

    xf = device(lax.rem(x0 + d + NX, NX), z0, h, c)
    xb = device(xprev, z0, h, c)
    zw = (device(x0, lax.rem(z0 + d + NZ, NZ), h, c), device(x0, lax.rem(z0 - d + NZ, NZ), h, c))
    sib = device(x0, z0, h, 1 - c)
    far = device(x0, z0, 1 - h, c)
    cols = [(row, lax.rem(col + k, NCOL)) for k in range(1, NCOL)]

    def copy(src, dst, send, recv, to):
        return pltpu.make_async_remote_copy(
            src_ref=src, dst_ref=dst, send_sem=send, recv_sem=recv,
            device_id=to, device_id_type=MESH,
        )

    barrier = pltpu.get_barrier_semaphore()
    peers = [xf, xb, *zw, sib, far] + cols
    loads = [
        pltpu.make_async_copy(src, dst, in_s.at[k])
        for k, (src, dst) in enumerate(
            ((x_hbm, xv), (w_hbm, wv), (mask_hbm, mask), (gate_hbm, gv), (up_hbm, uv))
        )
    ]
    loads[0].start()
    for peer in peers:
        pl.semaphore_signal(barrier, inc=1, device_id=peer, device_id_type=MESH)
    for load in loads[1:]:
        load.start()
    loads[0].wait()
    xs = xv[...].astype(F32)
    data[c, x0, 0, h] = jnp.concatenate([xs[:, :HALF], xs[:, HALF:]], axis=0).astype(BF16)
    pl.semaphore_wait(barrier, len(peers))

    def zslot(way, s):
        if s == 0:
            return 0
        if s == STEPS:
            return NZ - 1
        return 2 * s - 1 + c if way == 0 else 2 * s - c

    def cut(i, core, xsel, rsel):
        whose, _, lane, n = STREAMS[i]
        return data.at[core, xsel, rsel, h if whose == 0 else 1 - h, :, pl.ds(lane, n)]

    def span(g):
        lo, hi = slots(g)
        return pl.ds(lo, hi - lo)

    def describe(msg):
        kind = msg[0]
        if kind == "far":
            ref = data.at[c, x0, 0, h]
            return copy(ref, ref, far_s, far_r, far)
        if kind == "hid":
            ref = hs.at[col]
            return copy(ref, ref, h_s, h_r.at[msg[1]], cols[msg[1]])
        if kind == "part":
            _, g, k = msg
            src = pbuf.at[lax.rem(col + k + 1, NCOL), span(g)]
            return copy(src, rbuf.at[k, span(g)], p_s, p_r, cols[k])
        if kind == "z":
            _, i, way, s = msg
            xsel = x0 if STREAMS[i][1] == "zx" else slice(None)
            src, dst = cut(i, c, xsel, zslot(way, s - 1)), cut(i, c, xsel, zslot(way, s))
            return copy(src, dst, z_s.at[i], z_r.at[i, way * STEPS + s - 1], zw[way])
        if kind == "x":
            _, i, g, k = msg
            ref = cut(i, c, xprev if k == 1 else x0, span(g))
            return copy(ref, ref, x_s.at[i], x_r.at[i, 3 * g + k], xb if k == 2 else xf)
        _, i, g = msg
        ref = cut(i, c, slice(None), span(g))
        return copy(ref, ref, sib_s, sib_r.at[g], sib)

    def compute(g):
        ref = data.at[1 - c, :, span(g)]
        copy(ref, ref, sib_s, sib_r.at[g], sib).wait_recv()
        lo, hi = slots(g)
        nr = hi - lo
        tokens = NX * nr * NH * PACK
        hid = hs[:, lo:hi].astype(F32).reshape(NX, nr, NH, NC, TOK, BLK)
        blocks = [data[cc, :, lo:hi].reshape(tokens, HALF) for cc in range(NC)]
        terms, hids = [], []
        for cc in range(NC):
            t = lax.dot_general(
                blocks[cc], wm[...], (((1,), (1,)), ((), ())), preferred_element_type=F32
            ).reshape(NX, nr, NH, 2, TOK, 2 * BLK)
            terms.append(t[:, :, :, 0, :, :BLK] + t[:, :, :, 1, :, BLK:])
            v = hid[:, :, :, cc]
            zero = jnp.zeros_like(v)
            both = jnp.concatenate(
                [jnp.concatenate([v, zero], axis=-1), jnp.concatenate([zero, v], axis=-1)], axis=-2
            )
            hids.append(both.reshape(tokens, 2 * BLK).astype(BF16))
        term = jnp.concatenate(terms, axis=-2).reshape(NX, nr, ROWS, BLK)
        tbuf[:, lo:hi] = term
        pbuf[:, lo:hi] = term.astype(BF16)
        for k in range(NCOL - 1):
            describe(("part", g, k)).start()
        t = lax.dot_general(
            jnp.concatenate(hids, axis=0), jnp.concatenate(blocks, axis=0),
            (((0,), (0,)), ((), ())), preferred_element_type=F32,
        )
        acc[...] = t if g == 0 else acc[...] + t

    places = []
    for r in range(NZ):
        z = lax.rem(z0 + slot_offset(r) + NZ, NZ)
        places.append(pl.ds(pl.multiple_of(z * ROWS, ROWS), ROWS))

    def prepare():
        loads[3].wait()
        loads[4].wait()
        for r in range(NZ):
            gate = gv[places[r], :].astype(F32)
            up = uv[places[r], :].astype(F32)
            hs[col, r] = (gate * jax.nn.sigmoid(gate) * up).astype(BF16)
        for k in range(NCOL - 1):
            describe(("hid", k)).start()
        loads[1].wait()
        loads[2].wait()
        for b in range(2 * HALF // BLK):
            part, at = divmod(b * BLK, HALF)
            scale = mask[0, b].astype(F32)
            value = wv[:, b * BLK:(b + 1) * BLK].astype(F32) * scale
            wm[part * BLK:(part + 1) * BLK, at:at + BLK] = value.astype(BF16)

    describe(("far",)).start()
    for op in make_plan()[0]:
        if op[0] == "prepare":
            prepare()
        elif op[0] == "compute":
            compute(op[1])
        elif op[0] == "start":
            describe(op[1]).start()
        elif op[1][0] == "hid":
            for k in range(NCOL - 1):
                describe(("hid", k)).wait_recv()
        else:
            describe(op[1]).wait_recv()

    for b in range(2 * HALF // BLK):
        part, at = divmod(b * BLK, HALF)
        scale = mask[0, b].astype(F32)
        value = acc[part * BLK:(part + 1) * BLK, at:at + BLK] * scale
        gd_ref[:, b * BLK:(b + 1) * BLK] = value.astype(BF16)
    copy(rbuf, rbuf, p_s, p_r, sib).wait_recv()
    for r in range(NZ):
        gate = gv[places[r], :].astype(F32)
        up = uv[places[r], :].astype(F32)
        sig = jax.nn.sigmoid(gate)
        gh = tbuf[col, r]
        for k in range(NCOL - 1):
            gh = gh + rbuf[k, r].astype(F32)
        gu_ref[places[r], :] = (gh * gate * sig).astype(BF16)
        gg_ref[places[r], :] = (gh * up * sig * (1.0 + gate * (1.0 - sig))).astype(BF16)

    describe(("far",)).wait_send()
    for i, (_, order, _, _) in enumerate(STREAMS):
        zref = cut(i, c, 0 if order == "zx" else slice(None), pl.ds(0, NZ - 1))
        copy(zref, zref, z_s.at[i], z_r.at[i, 0], sib).wait_send()
        xref = cut(i, c, pl.ds(0, 3), pl.ds(0, NZ) if order == "zx" else 0)
        copy(xref, xref, x_s.at[i], x_r.at[i, 0], sib).wait_send()
    half = data.at[c]
    copy(half, half, sib_s, sib_r.at[0], sib).wait_send()
    three = hs.at[pl.ds(0, NCOL - 1)]
    copy(three, three, h_s, h_r.at[0], sib).wait_send()
    copy(rbuf, rbuf, p_s, p_r, sib).wait_send()


def shards(out_grad, down_weight, block_mask, gate_act, up_act):
    vmem = pl.BlockSpec(memory_space=pltpu.VMEM)
    hbm = pl.BlockSpec(memory_space=pl.ANY)
    dma = pltpu.SemaphoreType.DMA
    units = down_weight.shape[0]
    n = len(STREAMS)
    scratch = [
        pltpu.VMEM(out_grad.shape, BF16),
        pltpu.VMEM(down_weight.shape, BF16),
        pltpu.SMEM(block_mask.shape, jnp.int32),
        pltpu.VMEM(gate_act.shape, BF16),
        pltpu.VMEM(up_act.shape, BF16),
        pltpu.VMEM((NC, NX, NZ, NH, PACK, HALF), BF16),
        pltpu.VMEM((2 * units, HALF), BF16),
        pltpu.VMEM((NX, NZ, ROWS, units), BF16),
        pltpu.VMEM((2 * units, HALF), F32),
        pltpu.VMEM((NX, NZ, ROWS, units), F32),
        pltpu.VMEM((NX, NZ, ROWS, units), BF16),
        pltpu.VMEM((NCOL - 1, NZ, ROWS, units), BF16),
        dma((5,)), dma, dma, dma((n,)), dma((n, 2 * STEPS)), dma((n,)), dma((n, 3 * GROUPS)),
        dma, dma((GROUPS,)), dma, dma((NCOL - 1,)), dma, dma,
    ]
    return pl.pallas_call(
        kernel,
        out_shape=(
            jax.ShapeDtypeStruct(gate_act.shape, BF16),
            jax.ShapeDtypeStruct(up_act.shape, BF16),
            jax.ShapeDtypeStruct(down_weight.shape, BF16),
        ),
        in_specs=[hbm] * 5,
        out_specs=(vmem, vmem, vmem),
        scratch_shapes=scratch,
        compiler_params=pltpu.CompilerParams(
            collective_id=0, has_side_effects=True, vmem_limit_bytes=56 * 1024 * 1024
        ),
    )(out_grad, down_weight, block_mask, gate_act, up_act)


def solution(mesh):
    in_specs = (P("row", "col"), P("row", "col"), P("row", "col"), P("col", "row"), P("col", "row"))
    out_specs = (P("col", "row"), P("col", "row"), P("row", "col"))
    return jax.shard_map(shards, mesh=mesh, in_specs=in_specs, out_specs=out_specs, check_vma=False)
```

time: 277 us -> 71.4 us (0.26)
  waiting for transfers between devices: 233 us -> 0 us
  Pallas kernels: 0 us -> 66.4 us
  between operations: 14.1 us -> 0.65 us
  blocking collectives: 12.8 us -> 0 us
  matrix products: 10.6 us -> 0 us
    all_gather x1 -> x0, waiting for transfers between devices: 208 us -> none  [shards(): piece = lax.all_gather(out_grad, 'row', axis=0, tiled=True)]
    pallas_call x0 -> x1, Pallas kernels: none -> 66.4 us  [shards(): pl.pallas_call(kernel, out_shape=(jax.ShapeDtypeStruct(gate_act.shape, BF...]
    reduce_scatter x1 -> x0, waiting for transfers between devices: 25.1 us -> none  [shards(): lax.psum_scatter(partial_value, 'col', scatter_dimension=0, tiled=True)]
    all_gather x1 -> x0, blocking collectives: 12.8 us -> none  [shards(): all_hidden = lax.all_gather(hidden, 'col', axis=0, tiled=True)]
    dot_general x2 -> x0, matrix products: 10.6 us -> none  [the longest x1 6.05 us: shards(): lax.dot_general(piece, kept, (((1,), (1,)), ((), ())), preferred_element_...]
  transfers between devices with their start and end apart: 2 -> 0, of which waited for: 2 -> 0; matrix products, arithmetic and copies ran while one was open for 0% -> 0% of each run, Pallas kernels for 0% -> 0%
where the time goes in v2:
time: 71.4 us; the launch traced here: 71.2 us
  Pallas kernels  66.4 us (93%)
  local copies, waits for them, and re-layouts  4.1 us (6%)
    pallas_call x1, Pallas kernels, shards(): pl.pallas_call(kernel, out_shape=(jax.ShapeDtypeStruct(gate_act.shape, BF...  66.4 us
    unnamed x5, local copies, waits for them, and re-layouts  4.1 us

profile of v2, /device:TPU:1, one launch (start us, length us, event | category | flops | bytes accessed | tf_op | source)
XLA Modules:
  0.0 71.2 jit_solution(1827594547440588785)
XLA Ops:
  0.6 66.4 %shard_map.76 = (bf16[384,128]{1,0:T(8,128)(2,1)}, bf16[384,128]{1,0:T(8,128)(2,1)}, bf16[128,2048]{1,0:T(8,128)(2,1)}) custom-call(bf16[8,2048]{1,0:T(8,128)(2,1)} %x_hbm.1, bf16[128,2048]{1,0:T(8,128)(2,1)} %w_hbm.1, s32[1,16]{1,0:T(1,128)} %mask_hbm.1, bf16[384,128]{1,0:T(8,128)(2,1)} %gate_hbm.1, bf16[384,128]{1,0:T(8,128)(2,1)} %up_hbm.1), custom_call_target="tpu_custom_call" | custom-call | tf_op jit(solution)/shard_map/pallas_call | solution.py:348
  67.1 0.0 copy-start
  67.1 1.6 %copy.11 = bf16[384,128]{1,0:T(8,128)(2,1)} copy(bf16[384,128]{1,0:T(8,128)(2,1)} %get-tuple-element.6) | data formatting | bytes 196608
  68.7 0.0 copy-done
  68.7 0.6 copy.12
  69.3 1.9 %copy.13 = bf16[128,2048]{1,0:T(8,128)(2,1)} copy(bf16[128,2048]{1,0:T(8,128)(2,1)} %get-tuple-element.8) | data formatting | bytes 1048576
Async XLA Ops:
  67.1 1.6 %copy-start = (bf16[384,128]{1,0:T(8,128)(2,1)S(1)}, bf16[384,128]{1,0:T(8,128)(2,1)}, u32[]{:S(2)}) copy-start(bf16[384,128]{1,0:T(8,128)(2,1)} %get-tuple-element.7) | copy-start | bytes 294916

commit v3 on v2

--- a/solution.py
+++ b/solution.py
@@ -18,23 +18,23 @@
 HALF = 1024
 ROWS = NH * NC * TOK
 STEPS = NZ // 2
-GROUPS = STEPS + 1
+GROUPS = ((0, 1), (1, 5), (5, 9), (9, 12))
+VMEM_LIMIT = 56 * 1024 * 1024
 WAYS = (STEPS, STEPS - 1)
 
 STREAMS = (
-    (0, "zx", 384, 640),
-    (0, "xz", 0, 384),
-    (1, "zx", 384, 640),
-    (1, "xz", 0, 384),
+    (0, "zx", 256, 768),
+    (0, "xz", 0, 256),
+    (1, "zx", 256, 768),
+    (1, "xz", 0, 256),
 )
 
 
+XCOUNT = [3 * len(GROUPS) if order == "zx" else 3 for _, order, _, _ in STREAMS]
+
+
 def slots(g):
-    if g == 0:
-        return 0, 1
-    if g == STEPS:
-        return NZ - 1, NZ
-    return 2 * g - 1, 2 * g + 1
+    return GROUPS[g]
 
 
 def slot_offset(r):
@@ -46,22 +46,29 @@
     return -s if r % 2 else s
 
 
-def make_plan():
-    rate = {"z": 91e3, "x": 91e3, "sib": 400e3}
+def group_of(s):
+    lo = 2 * s - 1
+    g = next(g for g, (a, b) in enumerate(GROUPS) if a <= lo < b)
+    return g, GROUPS[g][1] - GROUPS[g][0]
+
+
+def make_plan(latency=3.2, hidden_at=16.0, slack=1.0, far_at=5.0):
+    rate = {"z": 91e3, "x": 91e3, "sib": 300e3}
     free = {"z": 0.0, "x": 0.0, "sib": 0.0}
-    latency, issue = 0.9, 0.06
+    issue, product = 0.08, 0.6
     ops, arrivals = [], []
     now = 0.0
     seen = {}
-    ready = [0] * GROUPS
+    ready = [0] * len(GROUPS)
     todo = []
 
-    def start(msg, kind, size):
+    def start(msg, kind, size, hops=1):
         nonlocal now
         ops.append(("start", msg))
         now += issue
-        free[kind] = max(free[kind], now) + size / rate[kind]
-        heapq.heappush(arrivals, (free[kind] + latency, msg))
+        free[kind] = max(free[kind], now) + size * hops / rate[kind]
+        late = latency if kind != "sib" else 1.0 + slack
+        heapq.heappush(arrivals, (free[kind] + late, msg))
 
     def size(i, slots_, xs):
         return slots_ * xs * PACK * STREAMS[i][3] * 2
@@ -70,72 +77,84 @@
         lo, hi = slots(g)
         return hi - lo
 
-    def send_z(i, way, s):
-        start(("z", i, way, s), "z", size(i, 1, 1 if STREAMS[i][1] == "zx" else NX))
+    def send_z(i, s, ways=(0, 1)):
+        for t in (s + 2, s + 1):
+            for way in ways:
+                if t <= WAYS[way]:
+                    xs = 1 if STREAMS[i][1] == "zx" else NX
+                    start(("z", i, way, t), "z", size(i, 1, xs), t - s)
 
     def send_x(i, g, k):
         start(("x", i, g, k), "x", size(i, nslots(g), 1))
 
-    def send_sib(i, g):
-        start(("sib", i, g), "sib", size(i, nslots(g), NX))
+    def send_sib(i, g, k):
+        start(("sib", i, g, k), "sib", size(i, nslots(g), NX if k is None else 1))
 
     def begin(i):
         if STREAMS[i][1] == "zx":
-            send_z(i, 0, 1)
-            send_z(i, 1, 1)
+            send_z(i, 0)
         send_x(i, 0, 0)
         send_x(i, 0, 2)
+        if STREAMS[i][1] == "zx":
+            send_sib(i, 0, 3)
 
     def count(key, full):
         seen[key] = seen.get(key, 0) + 1
         return seen[key] == full
 
-    for i in (0, 1):
-        begin(i)
+    for i, stream in enumerate(STREAMS):
+        if stream[0] == 0:
+            begin(i)
     ops.append(("prepare",))
     now += 1.5
-    heapq.heappush(arrivals, (5.5, ("far",)))
-    heapq.heappush(arrivals, (9.0, ("hid",)))
-    done = 0
+    heapq.heappush(arrivals, (far_at, ("far",)))
+    heapq.heappush(arrivals, (hidden_at, ("hid",)))
+    pieces = sum(4 if order == "zx" else 1 for _, order, _, _ in STREAMS)
+    late = []
     while arrivals or todo:
         if todo and (not arrivals or arrivals[0][0] > now):
-            g = todo.pop(0)
-            ops.append(("compute", g))
-            now += 0.6 if g in (0, STEPS) else 1.0
+            todo.sort(key=lambda task: task[0] != "term")
+            ops.append(todo.pop(0))
+            now += product
             continue
         at, msg = heapq.heappop(arrivals)
         now = max(now, at) + issue
         if msg[0] == "sib":
-            ready[msg[2]] += 1
-            while done < GROUPS and ready[done] == len(STREAMS) and seen.get("hid"):
-                todo.append(done)
-                done += 1
+            g = msg[2]
+            ready[g] += 1
+            if ready[g] == pieces:
+                todo.append(("term", g))
+                (todo if seen.get("hid") else late).append(("wgrad", g))
             continue
         ops.append(("wait", msg))
         if msg[0] == "far":
-            for i in (2, 3):
-                begin(i)
+            for i, stream in enumerate(STREAMS):
+                if stream[0] == 1:
+                    begin(i)
         elif msg[0] == "hid":
             seen["hid"] = 1
+            todo += late
         elif msg[0] == "z":
             _, i, way, s = msg
-            if s < WAYS[way]:
-                send_z(i, way, s + 1)
-            if count(("z", i, s), 1 if s == STEPS else 2):
+            if s % 2 == 0:
+                send_z(i, s, (way,))
+            g, full = group_of(s)
+            if count(("z", i, g), full):
                 if STREAMS[i][1] == "zx":
-                    send_x(i, s, 0)
-                    send_x(i, s, 2)
+                    send_x(i, g, 0)
+                    send_x(i, g, 2)
+                    send_sib(i, g, 3)
                 else:
-                    send_sib(i, s)
+                    send_sib(i, g, None)
         else:
             _, i, g, k = msg
             if k == 0:
                 send_x(i, g, 1)
-            if count(("x", i, g), 3):
-                if STREAMS[i][1] == "xz":
-                    send_z(i, 0, 1)
-                    send_z(i, 1, 1)
-                send_sib(i, g)
+            if STREAMS[i][1] == "zx":
+                send_sib(i, g, k)
+            elif count(("x", i, g), 3):
+                send_z(i, 0)
+                send_sib(i, g, None)
     return ops, now
 
 
@@ -151,14 +170,14 @@
     z0 = lax.rem(row // (NC * NH), NZ)
     x0 = row // (NC * NH * NZ)
     d = 1 - 2 * c
-    xprev = lax.rem(x0 - d + NX, NX)
+    xprev, xnext = lax.rem(x0 - d + NX, NX), lax.rem(x0 + d + NX, NX)
 
     def device(x, z, hh, cc):
         return (((x * NZ + z) * NH + hh) * NC + cc, col)
 
-    xf = device(lax.rem(x0 + d + NX, NX), z0, h, c)
+    xf = device(xnext, z0, h, c)
     xb = device(xprev, z0, h, c)
-    zw = (device(x0, lax.rem(z0 + d + NZ, NZ), h, c), device(x0, lax.rem(z0 - d + NZ, NZ), h, c))
+    zw = [[device(x0, lax.rem(z0 + t * e + NZ, NZ), h, c) for t in (1, 2)] for e in (d, -d)]
     sib = device(x0, z0, h, 1 - c)
     far = device(x0, z0, 1 - h, c)
     cols = [(row, lax.rem(col + k, NCOL)) for k in range(1, NCOL)]
@@ -170,7 +189,7 @@
         )
 
     barrier = pltpu.get_barrier_semaphore()
-    peers = [xf, xb, *zw, sib, far] + cols
+    peers = [xf, xb, *zw[0], *zw[1], sib, far] + cols
     loads = [
         pltpu.make_async_copy(src, dst, in_s.at[k])
         for k, (src, dst) in enumerate(
@@ -202,6 +221,8 @@
         lo, hi = slots(g)
         return pl.ds(lo, hi - lo)
 
+    xsem = [sum(XCOUNT[:i]) for i in range(len(STREAMS))]
+
     def describe(msg):
         kind = msg[0]
         if kind == "far":
@@ -217,46 +238,57 @@
         if kind == "z":
             _, i, way, s = msg
             xsel = x0 if STREAMS[i][1] == "zx" else slice(None)
-            src, dst = cut(i, c, xsel, zslot(way, s - 1)), cut(i, c, xsel, zslot(way, s))
-            return copy(src, dst, z_s.at[i], z_r.at[i, way * STEPS + s - 1], zw[way])
+            hops = 2 - s % 2
+            src, dst = cut(i, c, xsel, zslot(way, s - hops)), cut(i, c, xsel, zslot(way, s))
+            return copy(src, dst, z_s.at[i], z_r.at[i, way * STEPS + s - 1], zw[way][hops - 1])
         if kind == "x":
             _, i, g, k = msg
             ref = cut(i, c, xprev if k == 1 else x0, span(g))
-            return copy(ref, ref, x_s.at[i], x_r.at[i, 3 * g + k], xb if k == 2 else xf)
-        _, i, g = msg
-        ref = cut(i, c, slice(None), span(g))
+            return copy(ref, ref, x_s.at[i], x_r.at[xsem[i] + 3 * g + k], xb if k == 2 else xf)
+        _, i, g, k = msg
+        xsel = slice(None) if k is None else (xprev, lax.rem(x0 + 2, NX), xnext, x0)[k]
+        ref = cut(i, c, xsel, span(g))
         return copy(ref, ref, sib_s, sib_r.at[g], sib)
 
-    def compute(g):
+    def blocks(g):
+        lo, hi = slots(g)
+        return [data[cc, :, lo:hi].reshape(NX * (hi - lo) * NH * PACK, HALF) for cc in range(NC)]
+
+    def term(g):
         ref = data.at[1 - c, :, span(g)]
         copy(ref, ref, sib_s, sib_r.at[g], sib).wait_recv()
         lo, hi = slots(g)
-        nr = hi - lo
-        tokens = NX * nr * NH * PACK
-        hid = hs[:, lo:hi].astype(F32).reshape(NX, nr, NH, NC, TOK, BLK)
-        blocks = [data[cc, :, lo:hi].reshape(tokens, HALF) for cc in range(NC)]
-        terms, hids = [], []
+        terms = []
+        for block in blocks(g):
+            t = lax.dot_general(
+                block, wm[...], (((1,), (1,)), ((), ())), preferred_element_type=F32
+            ).reshape(NX, hi - lo, NH, 2, TOK, 2 * BLK)
+            terms.append(t[:, :, :, 0, :, :BLK] + t[:, :, :, 1, :, BLK:])
+        value = jnp.concatenate(terms, axis=-2).reshape(NX, hi - lo, ROWS, BLK)
+        tbuf[:, lo:hi] = value
+        pbuf[:, lo:hi] = value.astype(BF16)
+        for k in range(NCOL - 1):
+            describe(("part", g, k)).start()
+
+    started = []
+
+    def wgrad(g):
+        lo, hi = slots(g)
+        hid = hs[:, lo:hi].astype(F32).reshape(NX, hi - lo, NH, NC, TOK, BLK)
+        hids = []
         for cc in range(NC):
-            t = lax.dot_general(
-                blocks[cc], wm[...], (((1,), (1,)), ((), ())), preferred_element_type=F32
-            ).reshape(NX, nr, NH, 2, TOK, 2 * BLK)
-            terms.append(t[:, :, :, 0, :, :BLK] + t[:, :, :, 1, :, BLK:])
             v = hid[:, :, :, cc]
             zero = jnp.zeros_like(v)
             both = jnp.concatenate(
                 [jnp.concatenate([v, zero], axis=-1), jnp.concatenate([zero, v], axis=-1)], axis=-2
             )
-            hids.append(both.reshape(tokens, 2 * BLK).astype(BF16))
-        term = jnp.concatenate(terms, axis=-2).reshape(NX, nr, ROWS, BLK)
-        tbuf[:, lo:hi] = term
-        pbuf[:, lo:hi] = term.astype(BF16)
-        for k in range(NCOL - 1):
-            describe(("part", g, k)).start()
+            hids.append(both.reshape(-1, 2 * BLK).astype(BF16))
         t = lax.dot_general(
-            jnp.concatenate(hids, axis=0), jnp.concatenate(blocks, axis=0),
+            jnp.concatenate(hids, axis=0), jnp.concatenate(blocks(g), axis=0),
             (((0,), (0,)), ((), ())), preferred_element_type=F32,
         )
-        acc[...] = t if g == 0 else acc[...] + t
+        acc[...] = acc[...] + t if started else t
+        started.append(g)
 
     places = []
     for r in range(NZ):
@@ -284,8 +316,10 @@
     for op in make_plan()[0]:
         if op[0] == "prepare":
             prepare()
-        elif op[0] == "compute":
-            compute(op[1])
+        elif op[0] == "term":
+            term(op[1])
+        elif op[0] == "wgrad":
+            wgrad(op[1])
         elif op[0] == "start":
             describe(op[1]).start()
         elif op[1][0] == "hid":
@@ -315,7 +349,7 @@
         zref = cut(i, c, 0 if order == "zx" else slice(None), pl.ds(0, NZ - 1))
         copy(zref, zref, z_s.at[i], z_r.at[i, 0], sib).wait_send()
         xref = cut(i, c, pl.ds(0, 3), pl.ds(0, NZ) if order == "zx" else 0)
-        copy(xref, xref, x_s.at[i], x_r.at[i, 0], sib).wait_send()
+        copy(xref, xref, x_s.at[i], x_r.at[0], sib).wait_send()
     half = data.at[c]
     copy(half, half, sib_s, sib_r.at[0], sib).wait_send()
     three = hs.at[pl.ds(0, NCOL - 1)]
@@ -329,6 +363,7 @@
     dma = pltpu.SemaphoreType.DMA
     units = down_weight.shape[0]
     n = len(STREAMS)
+    xcount = sum(XCOUNT)
     scratch = [
         pltpu.VMEM(out_grad.shape, BF16),
         pltpu.VMEM(down_weight.shape, BF16),
@@ -342,21 +377,22 @@
         pltpu.VMEM((NX, NZ, ROWS, units), F32),
         pltpu.VMEM((NX, NZ, ROWS, units), BF16),
         pltpu.VMEM((NCOL - 1, NZ, ROWS, units), BF16),
-        dma((5,)), dma, dma, dma((n,)), dma((n, 2 * STEPS)), dma((n,)), dma((n, 3 * GROUPS)),
-        dma, dma((GROUPS,)), dma, dma((NCOL - 1,)), dma, dma,
+        dma((5,)), dma, dma, dma((n,)), dma((n, 2 * STEPS - 1)), dma((n,)), dma((xcount,)),
+        dma, dma((len(GROUPS),)), dma, dma((NCOL - 1,)), dma, dma,
     ]
+    out_shape = (
+        jax.ShapeDtypeStruct(gate_act.shape, BF16),
+        jax.ShapeDtypeStruct(up_act.shape, BF16),
+        jax.ShapeDtypeStruct(down_weight.shape, BF16),
+    )
     return pl.pallas_call(
         kernel,
-        out_shape=(
-            jax.ShapeDtypeStruct(gate_act.shape, BF16),
-            jax.ShapeDtypeStruct(up_act.shape, BF16),
-            jax.ShapeDtypeStruct(down_weight.shape, BF16),
-        ),
+        out_shape=out_shape,
         in_specs=[hbm] * 5,
         out_specs=(vmem, vmem, vmem),
         scratch_shapes=scratch,
         compiler_params=pltpu.CompilerParams(
-            collective_id=0, has_side_effects=True, vmem_limit_bytes=56 * 1024 * 1024
+            collective_id=0, has_side_effects=True, vmem_limit_bytes=VMEM_LIMIT
         ),
     )(out_grad, down_weight, block_mask, gate_act, up_act)
 

time: 71.4 us -> 60.8 us (0.85)
  Pallas kernels: 66.4 us -> 55.9 us
    pallas_call x1, Pallas kernels: 66.4 us -> 55.9 us  [shards(): pl.pallas_call(kernel, out_shape=out_shape, in_specs=[hbm] * 5, out_specs...]
where the time goes in v3:
time: 60.8 us; the launch traced here: 60.6 us
  Pallas kernels  55.9 us (92%)
  local copies, waits for them, and re-layouts  4.1 us (7%)
  between operations  0.65 us (1%)
    pallas_call x1, Pallas kernels, shards(): pl.pallas_call(kernel, out_shape=out_shape, in_specs=[hbm] * 5, out_specs...  55.9 us
    unnamed x5, local copies, waits for them, and re-layouts  4.1 us

profile of v3, /device:TPU:1, one launch (start us, length us, event | category | flops | bytes accessed | tf_op | source)
XLA Modules:
  0.0 60.6 jit_solution(7222555852699482757)
XLA Ops:
  0.6 55.9 %shard_map.76 = (bf16[384,128]{1,0:T(8,128)(2,1)}, bf16[384,128]{1,0:T(8,128)(2,1)}, bf16[128,2048]{1,0:T(8,128)(2,1)}) custom-call(bf16[8,2048]{1,0:T(8,128)(2,1)} %x_hbm.1, bf16[128,2048]{1,0:T(8,128)(2,1)} %w_hbm.1, s32[1,16]{1,0:T(1,128)} %mask_hbm.1, bf16[384,128]{1,0:T(8,128)(2,1)} %gate_hbm.1, bf16[384,128]{1,0:T(8,128)(2,1)} %up_hbm.1), custom_call_target="tpu_custom_call" | custom-call | tf_op jit(solution)/shard_map/pallas_call | solution.py:388
  56.5 0.0 copy-start
  56.5 1.6 %copy.11 = bf16[384,128]{1,0:T(8,128)(2,1)} copy(bf16[384,128]{1,0:T(8,128)(2,1)} %get-tuple-element.6) | data formatting | bytes 196608
  58.1 0.0 copy-done
  58.1 0.6 %copy.12 = bf16[384,128]{1,0:T(8,128)(2,1)} copy(bf16[384,128]{1,0:T(8,128)(2,1)S(1)} %copy-done) | data formatting | bytes 196608
  58.7 1.9 %copy.13 = bf16[128,2048]{1,0:T(8,128)(2,1)} copy(bf16[128,2048]{1,0:T(8,128)(2,1)} %get-tuple-element.8) | data formatting | bytes 1048576
Async XLA Ops:
  56.5 1.6 %copy-start = (bf16[384,128]{1,0:T(8,128)(2,1)S(1)}, bf16[384,128]{1,0:T(8,128)(2,1)}, u32[]{:S(2)}) copy-start(bf16[384,128]{1,0:T(8,128)(2,1)} %get-tuple-element.7) | copy-start | bytes 294916

commit v4 on v3

--- a/solution.py
+++ b/solution.py
@@ -18,19 +18,21 @@
 HALF = 1024
 ROWS = NH * NC * TOK
 STEPS = NZ // 2
-GROUPS = ((0, 1), (1, 5), (5, 9), (9, 12))
+GROUPS = ((0, 1), (1, 3), (3, 5), (5, 7), (7, 9), (9, 11), (11, 12))
 VMEM_LIMIT = 56 * 1024 * 1024
 WAYS = (STEPS, STEPS - 1)
 
+RING = (0, 1, 2, 3, 4, 5)
+SKIP = (0, 0, 2, 2, 4, 4)
+MIXED = (0, 0, 2, 2, 4, 5)
+
 STREAMS = (
-    (0, "zx", 256, 768),
-    (0, "xz", 0, 256),
-    (1, "zx", 256, 768),
-    (1, "xz", 0, 256),
+    (0, "zx", 256, 768, MIXED),
+    (0, "xz", 0, 256, RING),
+    (1, "zx", 256, 768, SKIP),
+    (1, "xz", 0, 256, SKIP),
 )
-
-
-XCOUNT = [3 * len(GROUPS) if order == "zx" else 3 for _, order, _, _ in STREAMS]
+XCOUNT = [3 * len(GROUPS) if order == "zx" else 3 for _, order, _, _, _ in STREAMS]
 
 
 def slots(g):
@@ -52,10 +54,10 @@
     return g, GROUPS[g][1] - GROUPS[g][0]
 
 
-def make_plan(latency=3.2, hidden_at=16.0, slack=1.0, far_at=5.0):
+def make_plan(latency=3.2, hidden_at=16.0, slack=0.5, far_at=5.0):
     rate = {"z": 91e3, "x": 91e3, "sib": 300e3}
     free = {"z": 0.0, "x": 0.0, "sib": 0.0}
-    issue, product = 0.08, 0.6
+    issue = 0.02
     ops, arrivals = [], []
     now = 0.0
     seen = {}
@@ -78,9 +80,9 @@
         return hi - lo
 
     def send_z(i, s, ways=(0, 1)):
-        for t in (s + 2, s + 1):
+        for t in range(STEPS, 0, -1):
             for way in ways:
-                if t <= WAYS[way]:
+                if STREAMS[i][4][t - 1] == s and t <= WAYS[way]:
                     xs = 1 if STREAMS[i][1] == "zx" else NX
                     start(("z", i, way, t), "z", size(i, 1, xs), t - s)
 
@@ -106,16 +108,16 @@
         if stream[0] == 0:
             begin(i)
     ops.append(("prepare",))
-    now += 1.5
+    now += 1.0
     heapq.heappush(arrivals, (far_at, ("far",)))
     heapq.heappush(arrivals, (hidden_at, ("hid",)))
-    pieces = sum(4 if order == "zx" else 1 for _, order, _, _ in STREAMS)
+    pieces = sum(4 if order == "zx" else 1 for _, order, _, _, _ in STREAMS)
     late = []
     while arrivals or todo:
         if todo and (not arrivals or arrivals[0][0] > now):
             todo.sort(key=lambda task: task[0] != "term")
             ops.append(todo.pop(0))
-            now += product
+            now += 0.1 + 0.08 * nslots(ops[-1][1])
             continue
         at, msg = heapq.heappop(arrivals)
         now = max(now, at) + issue
@@ -128,6 +130,7 @@
             continue
         ops.append(("wait", msg))
         if msg[0] == "far":
+            ops.extend(("start", ("hid", k)) for k in range(NCOL - 1))
             for i, stream in enumerate(STREAMS):
                 if stream[0] == 1:
                     begin(i)
@@ -136,8 +139,7 @@
             todo += late
         elif msg[0] == "z":
             _, i, way, s = msg
-            if s % 2 == 0:
-                send_z(i, s, (way,))
+            send_z(i, s, (way,))
             g, full = group_of(s)
             if count(("z", i, g), full):
                 if STREAMS[i][1] == "zx":
@@ -214,7 +216,7 @@
         return 2 * s - 1 + c if way == 0 else 2 * s - c
 
     def cut(i, core, xsel, rsel):
-        whose, _, lane, n = STREAMS[i]
+        whose, _, lane, n, _ = STREAMS[i]
         return data.at[core, xsel, rsel, h if whose == 0 else 1 - h, :, pl.ds(lane, n)]
 
     def span(g):
@@ -238,7 +240,7 @@
         if kind == "z":
             _, i, way, s = msg
             xsel = x0 if STREAMS[i][1] == "zx" else slice(None)
-            hops = 2 - s % 2
+            hops = s - STREAMS[i][4][s - 1]
             src, dst = cut(i, c, xsel, zslot(way, s - hops)), cut(i, c, xsel, zslot(way, s))
             return copy(src, dst, z_s.at[i], z_r.at[i, way * STEPS + s - 1], zw[way][hops - 1])
         if kind == "x":
@@ -302,8 +304,6 @@
             gate = gv[places[r], :].astype(F32)
             up = uv[places[r], :].astype(F32)
             hs[col, r] = (gate * jax.nn.sigmoid(gate) * up).astype(BF16)
-        for k in range(NCOL - 1):
-            describe(("hid", k)).start()
         loads[1].wait()
         loads[2].wait()
         for b in range(2 * HALF // BLK):
@@ -345,7 +345,7 @@
         gg_ref[places[r], :] = (gh * up * sig * (1.0 + gate * (1.0 - sig))).astype(BF16)
 
     describe(("far",)).wait_send()
-    for i, (_, order, _, _) in enumerate(STREAMS):
+    for i, (_, order, _, _, _) in enumerate(STREAMS):
         zref = cut(i, c, 0 if order == "zx" else slice(None), pl.ds(0, NZ - 1))
         copy(zref, zref, z_s.at[i], z_r.at[i, 0], sib).wait_send()
         xref = cut(i, c, pl.ds(0, 3), pl.ds(0, NZ) if order == "zx" else 0)
@@ -355,6 +355,11 @@
     three = hs.at[pl.ds(0, NCOL - 1)]
     copy(three, three, h_s, h_r.at[0], sib).wait_send()
     copy(rbuf, rbuf, p_s, p_r, sib).wait_send()
+
+
+def hand_over(*refs):
+    for src, dst in zip(refs[:3], refs[3:]):
+        dst[...] = src[...]
 
 
 def shards(out_grad, down_weight, block_mask, gate_act, up_act):
@@ -385,7 +390,7 @@
         jax.ShapeDtypeStruct(up_act.shape, BF16),
         jax.ShapeDtypeStruct(down_weight.shape, BF16),
     )
-    return pl.pallas_call(
+    results = pl.pallas_call(
         kernel,
         out_shape=out_shape,
         in_specs=[hbm] * 5,
@@ -395,6 +400,13 @@
             collective_id=0, has_side_effects=True, vmem_limit_bytes=VMEM_LIMIT
         ),
     )(out_grad, down_weight, block_mask, gate_act, up_act)
+    return pl.pallas_call(
+        hand_over,
+        out_shape=out_shape,
+        in_specs=[vmem] * 3,
+        out_specs=(vmem,) * 3,
+        compiler_params=pltpu.CompilerParams(vmem_limit_bytes=VMEM_LIMIT),
+    )(*results)
 
 
 def solution(mesh):

time: 60.8 us -> 57.7 us (0.949)
  local copies, waits for them, and re-layouts: 4.1 us -> 0 us
  Pallas kernels: 55.9 us -> 56.8 us
    unnamed x5 -> x0, local copies, waits for them, and re-layouts: 4.1 us -> none
    pallas_call x0 -> x1, Pallas kernels: none -> 2.01 us  [shards(): pl.pallas_call(hand_over, out_shape=out_shape, in_specs=[vmem] * 3, out_s...]
    pallas_call x1, Pallas kernels: 55.9 us -> 54.8 us  [shards(): pl.pallas_call(kernel, out_shape=out_shape, in_specs=[hbm] * 5, out_specs...]
where the time goes in v4:
time: 57.7 us; the launch traced here: 57.5 us
  Pallas kernels  56.8 us (98%)
  between operations  0.64 us (1%)
    pallas_call x1, Pallas kernels, shards(): pl.pallas_call(kernel, out_shape=out_shape, in_specs=[hbm] * 5, out_specs...  54.8 us
    pallas_call x1, Pallas kernels, shards(): pl.pallas_call(hand_over, out_shape=out_shape, in_specs=[vmem] * 3, out_s...  2.01 us

profile of v4, /device:TPU:1, one launch (start us, length us, event | category | flops | bytes accessed | tf_op | source)
XLA Modules:
  0.0 57.5 jit_solution(4579511988740858865)
XLA Ops:
  0.6 54.8 %shard_map.76 = (bf16[384,128]{1,0:T(8,128)(2,1)}, bf16[384,128]{1,0:T(8,128)(2,1)}, bf16[128,2048]{1,0:T(8,128)(2,1)}) custom-call(bf16[8,2048]{1,0:T(8,128)(2,1)} %x_hbm.1, bf16[128,2048]{1,0:T(8,128)(2,1)} %w_hbm.1, s32[1,16]{1,0:T(1,128)} %mask_hbm.1, bf16[384,128]{1,0:T(8,128)(2,1)} %gate_hbm.1, bf16[384,128]{1,0:T(8,128)(2,1)} %up_hbm.1), custom_call_target="tpu_custom_call" | custom-call | tf_op jit(solution)/shard_map/pallas_call | solution.py:393
  55.5 2.0 %shard_map.77 = (bf16[384,128]{1,0:T(8,128)(2,1)}, bf16[384,128]{1,0:T(8,128)(2,1)}, bf16[128,2048]{1,0:T(8,128)(2,1)}) custom-call(bf16[384,128]{1,0:T(8,128)(2,1)} %get-tuple-element.6.refs_0_, bf16[384,128]{1,0:T(8,128)(2,1)} %get-tuple-element.7.refs_1_, bf16[128,2048]{1,0:T(8,128)(2,1)} %get-tuple-element.8.refs_2_), custom_call_target="tpu_custom_call" | custom-call | tf_op jit(solution)/shard_map/pallas_call | solution.py:403

commit v5 on v4

--- a/solution.py
+++ b/solution.py
@@ -24,11 +24,11 @@
 
 RING = (0, 1, 2, 3, 4, 5)
 SKIP = (0, 0, 2, 2, 4, 4)
-MIXED = (0, 0, 2, 2, 4, 5)
+MIXED = (0, 1, 2, 2, 4, 4)
 
 STREAMS = (
     (0, "zx", 256, 768, MIXED),
-    (0, "xz", 0, 256, RING),
+    (0, "xz", 0, 256, MIXED),
     (1, "zx", 256, 768, SKIP),
     (1, "xz", 0, 256, SKIP),
 )
@@ -54,9 +54,10 @@
     return g, GROUPS[g][1] - GROUPS[g][0]
 
 
-def make_plan(latency=3.2, hidden_at=16.0, slack=0.5, far_at=5.0):
-    rate = {"z": 91e3, "x": 91e3, "sib": 300e3}
+def make_plan(zlate=3.2, xlate=3.6, zrate=97e3, xrate=102e3, far_at=6.2, hidden_at=17.0, slack=1.4):
+    rate = {"z": zrate, "x": xrate, "sib": 300e3}
     free = {"z": 0.0, "x": 0.0, "sib": 0.0}
+    late = {"z": zlate, "x": xlate, "sib": 1.0 + slack}
     issue = 0.02
     ops, arrivals = [], []
     now = 0.0
@@ -69,8 +70,7 @@
         ops.append(("start", msg))
         now += issue
         free[kind] = max(free[kind], now) + size * hops / rate[kind]
-        late = latency if kind != "sib" else 1.0 + slack
-        heapq.heappush(arrivals, (free[kind] + late, msg))
+        heapq.heappush(arrivals, (free[kind] + late[kind], msg))
 
     def size(i, slots_, xs):
         return slots_ * xs * PACK * STREAMS[i][3] * 2
@@ -112,7 +112,7 @@
     heapq.heappush(arrivals, (far_at, ("far",)))
     heapq.heappush(arrivals, (hidden_at, ("hid",)))
     pieces = sum(4 if order == "zx" else 1 for _, order, _, _, _ in STREAMS)
-    late = []
+    waiting = []
     while arrivals or todo:
         if todo and (not arrivals or arrivals[0][0] > now):
             todo.sort(key=lambda task: task[0] != "term")
@@ -126,7 +126,7 @@
             ready[g] += 1
             if ready[g] == pieces:
                 todo.append(("term", g))
-                (todo if seen.get("hid") else late).append(("wgrad", g))
+                (todo if seen.get("hid") else waiting).append(("wgrad", g))
             continue
         ops.append(("wait", msg))
         if msg[0] == "far":
@@ -136,7 +136,7 @@
                     begin(i)
         elif msg[0] == "hid":
             seen["hid"] = 1
-            todo += late
+            todo += waiting
         elif msg[0] == "z":
             _, i, way, s = msg
             send_z(i, s, (way,))

time: 57.7 us -> 55.6 us (0.964)
  Pallas kernels: 56.8 us -> 54.8 us
    pallas_call x1, Pallas kernels: 54.8 us -> 52.8 us  [shards(): pl.pallas_call(kernel, out_shape=out_shape, in_specs=[hbm] * 5, out_specs...]
where the time goes in v5:
time: 55.6 us; the launch traced here: 55.4 us
  Pallas kernels  54.8 us (99%)
  between operations  0.64 us (1%)
    pallas_call x1, Pallas kernels, shards(): pl.pallas_call(kernel, out_shape=out_shape, in_specs=[hbm] * 5, out_specs...  52.8 us
    pallas_call x1, Pallas kernels, shards(): pl.pallas_call(hand_over, out_shape=out_shape, in_specs=[vmem] * 3, out_s...  2.01 us

profile of v5, /device:TPU:1, one launch (start us, length us, event | category | flops | bytes accessed | tf_op | source)
XLA Modules:
  0.0 55.4 jit_solution(18390264429868080049)
XLA Ops:
  0.6 52.8 %shard_map.76 = (bf16[384,128]{1,0:T(8,128)(2,1)}, bf16[384,128]{1,0:T(8,128)(2,1)}, bf16[128,2048]{1,0:T(8,128)(2,1)}) custom-call(bf16[8,2048]{1,0:T(8,128)(2,1)} %x_hbm.1, bf16[128,2048]{1,0:T(8,128)(2,1)} %w_hbm.1, s32[1,16]{1,0:T(1,128)} %mask_hbm.1, bf16[384,128]{1,0:T(8,128)(2,1)} %gate_hbm.1, bf16[384,128]{1,0:T(8,128)(2,1)} %up_hbm.1), custom_call_target="tpu_custom_call" | custom-call | tf_op jit(solution)/shard_map/pallas_call | solution.py:393
  53.4 2.0 %shard_map.77 = (bf16[384,128]{1,0:T(8,128)(2,1)}, bf16[384,128]{1,0:T(8,128)(2,1)}, bf16[128,2048]{1,0:T(8,128)(2,1)}) custom-call(bf16[384,128]{1,0:T(8,128)(2,1)} %get-tuple-element.6.refs_0_, bf16[384,128]{1,0:T(8,128)(2,1)} %get-tuple-element.7.refs_1_, bf16[128,2048]{1,0:T(8,128)(2,1)} %get-tuple-element.8.refs_2_), custom_call_target="tpu_custom_call" | custom-call | tf_op jit(solution)/shard_map/pallas_call | solution.py:403

commit v6 on v5

--- a/solution.py
+++ b/solution.py
@@ -20,6 +20,7 @@
 STEPS = NZ // 2
 GROUPS = ((0, 1), (1, 3), (3, 5), (5, 7), (7, 9), (9, 11), (11, 12))
 VMEM_LIMIT = 56 * 1024 * 1024
+PIECES = 2
 WAYS = (STEPS, STEPS - 1)
 
 RING = (0, 1, 2, 3, 4, 5)
@@ -54,7 +55,7 @@
     return g, GROUPS[g][1] - GROUPS[g][0]
 
 
-def make_plan(zlate=3.2, xlate=3.6, zrate=97e3, xrate=102e3, far_at=6.2, hidden_at=17.0, slack=1.4):
+def make_plan(zlate=3.2, xlate=3.62, zrate=97e3, xrate=102e3, far_at=5.76, hidden_at=20.9, slack=1.2):
     rate = {"z": zrate, "x": xrate, "sib": 300e3}
     free = {"z": 0.0, "x": 0.0, "sib": 0.0}
     late = {"z": zlate, "x": xlate, "sib": 1.0 + slack}
@@ -162,9 +163,9 @@
 
 def kernel(
     x_hbm, w_hbm, mask_hbm, gate_hbm, up_hbm,
-    gg_ref, gu_ref, gd_ref,
-    xv, wv, mask, gv, uv, data, wm, hs, acc, tbuf, pbuf, rbuf,
-    in_s, far_s, far_r, z_s, z_r, x_s, x_r, sib_s, sib_r, h_s, h_r, p_s, p_r,
+    gg_hbm, gu_hbm, gd_hbm,
+    xv, wv, mask, gv, uv, data, wm, hs, acc, tbuf, pbuf, rbuf, gg_ref, gu_ref, gd_ref,
+    in_s, far_s, far_r, z_s, z_r, x_s, x_r, sib_s, sib_r, h_s, h_r, p_s, p_r, out_s,
 ):
     row, col = lax.axis_index("row"), lax.axis_index("col")
     c = lax.rem(row, NC)
@@ -333,6 +334,11 @@
         scale = mask[0, b].astype(F32)
         value = acc[part * BLK:(part + 1) * BLK, at:at + BLK] * scale
         gd_ref[:, b * BLK:(b + 1) * BLK] = value.astype(BF16)
+    outs = [
+        pltpu.make_async_copy(src, dst, out_s.at[k])
+        for k, (src, dst) in enumerate(((gg_ref, gg_hbm), (gu_ref, gu_hbm), (gd_ref, gd_hbm)))
+    ]
+    outs[2].start()
     copy(rbuf, rbuf, p_s, p_r, sib).wait_recv()
     for r in range(NZ):
         gate = gv[places[r], :].astype(F32)
@@ -344,6 +350,8 @@
         gu_ref[places[r], :] = (gh * gate * sig).astype(BF16)
         gg_ref[places[r], :] = (gh * up * sig * (1.0 + gate * (1.0 - sig))).astype(BF16)
 
+    outs[0].start()
+    outs[1].start()
     describe(("far",)).wait_send()
     for i, (_, order, _, _, _) in enumerate(STREAMS):
         zref = cut(i, c, 0 if order == "zx" else slice(None), pl.ds(0, NZ - 1))
@@ -355,15 +363,30 @@
     three = hs.at[pl.ds(0, NCOL - 1)]
     copy(three, three, h_s, h_r.at[0], sib).wait_send()
     copy(rbuf, rbuf, p_s, p_r, sib).wait_send()
+    for out in outs:
+        out.wait()
 
 
 def hand_over(*refs):
-    for src, dst in zip(refs[:3], refs[3:]):
-        dst[...] = src[...]
+    sources, results, stages, sems = refs[:3], refs[3:6], refs[6:9], refs[9]
+    loads, stores = [], []
+    for src, dst, stage in zip(sources, results, stages):
+        rows = src.shape[0] // PIECES
+        for p in range(PIECES):
+            at = pl.ds(p * rows, rows)
+            n = len(loads)
+            loads.append(pltpu.make_async_copy(src.at[at], stage.at[at], sems.at[n]))
+            stores.append(pltpu.make_async_copy(stage.at[at], dst.at[at], sems.at[n]))
+    for load in loads:
+        load.start()
+    for load, store in zip(loads, stores):
+        load.wait()
+        store.start()
+    for store in stores:
+        store.wait()
 
 
 def shards(out_grad, down_weight, block_mask, gate_act, up_act):
-    vmem = pl.BlockSpec(memory_space=pltpu.VMEM)
     hbm = pl.BlockSpec(memory_space=pl.ANY)
     dma = pltpu.SemaphoreType.DMA
     units = down_weight.shape[0]
@@ -382,8 +405,11 @@
         pltpu.VMEM((NX, NZ, ROWS, units), F32),
         pltpu.VMEM((NX, NZ, ROWS, units), BF16),
         pltpu.VMEM((NCOL - 1, NZ, ROWS, units), BF16),
+        pltpu.VMEM(gate_act.shape, BF16),
+        pltpu.VMEM(up_act.shape, BF16),
+        pltpu.VMEM(down_weight.shape, BF16),
         dma((5,)), dma, dma, dma((n,)), dma((n, 2 * STEPS - 1)), dma((n,)), dma((xcount,)),
-        dma, dma((len(GROUPS),)), dma, dma((NCOL - 1,)), dma, dma,
+        dma, dma((len(GROUPS),)), dma, dma((NCOL - 1,)), dma, dma, dma((3,)),
     ]
     out_shape = (
         jax.ShapeDtypeStruct(gate_act.shape, BF16),
@@ -394,7 +420,7 @@
         kernel,
         out_shape=out_shape,
         in_specs=[hbm] * 5,
-        out_specs=(vmem, vmem, vmem),
+        out_specs=(hbm,) * 3,
         scratch_shapes=scratch,
         compiler_params=pltpu.CompilerParams(
             collective_id=0, has_side_effects=True, vmem_limit_bytes=VMEM_LIMIT
@@ -403,8 +429,9 @@
     return pl.pallas_call(
         hand_over,
         out_shape=out_shape,
-        in_specs=[vmem] * 3,
-        out_specs=(vmem,) * 3,
+        in_specs=[hbm] * 3,
+        out_specs=(hbm,) * 3,
+        scratch_shapes=[pltpu.VMEM(o.shape, BF16) for o in out_shape] + [dma((3 * PIECES,))],
         compiler_params=pltpu.CompilerParams(vmem_limit_bytes=VMEM_LIMIT),
     )(*results)
 

time: 55.6 us -> 55.3 us (level)
  no operation moved by 1% of the time
where the time goes in v6:
time: 55.3 us; the launch traced here: 55.2 us
  Pallas kernels  54.5 us (99%)
  between operations  0.64 us (1%)
    pallas_call x1, Pallas kernels, shards(): pl.pallas_call(kernel, out_shape=out_shape, in_specs=[hbm] * 5, out_specs...  52.6 us
    pallas_call x1, Pallas kernels, shards(): pl.pallas_call(hand_over, out_shape=out_shape, in_specs=[hbm] * 3, out_sp...  1.91 us

profile of v6, /device:TPU:1, one launch (start us, length us, event | category | flops | bytes accessed | tf_op | source)
XLA Modules:
  0.0 55.2 jit_solution(11728454460913441901)
XLA Ops:
  0.6 52.6 %shard_map.76 = (bf16[384,128]{1,0:T(8,128)(2,1)}, bf16[384,128]{1,0:T(8,128)(2,1)}, bf16[128,2048]{1,0:T(8,128)(2,1)}) custom-call(bf16[8,2048]{1,0:T(8,128)(2,1)} %x_hbm.1, bf16[128,2048]{1,0:T(8,128)(2,1)} %w_hbm.1, s32[1,16]{1,0:T(1,128)} %mask_hbm.1, bf16[384,128]{1,0:T(8,128)(2,1)} %gate_hbm.1, bf16[384,128]{1,0:T(8,128)(2,1)} %up_hbm.1), custom_call_target="tpu_custom_call" | custom-call | tf_op jit(solution)/shard_map/pallas_call | solution.py:419
  53.2 1.9 %shard_map.77 = (bf16[384,128]{1,0:T(8,128)(2,1)}, bf16[384,128]{1,0:T(8,128)(2,1)}, bf16[128,2048]{1,0:T(8,128)(2,1)}) custom-call(bf16[384,128]{1,0:T(8,128)(2,1)} %get-tuple-element.6.refs_0_, bf16[384,128]{1,0:T(8,128)(2,1)} %get-tuple-element.7.refs_1_, bf16[128,2048]{1,0:T(8,128)(2,1)} %get-tuple-element.8.refs_2_), custom_call_target="tpu_custom_call" | custom-call | tf_op jit(solution)/shard_map/pallas_call | solution.py:429
